TPU v7x, 256 devices: a whole 4x4x8 slice. The times are simulated.
256 devices in a mesh: ctx: 64 (over x, z, core), tp: 4 (over y).
Axes of the slice: x: 4, y: 4, z: 8, core: 2. Of those that a mesh axis runs over, the one named last changes fastest.
Arguments:
- queries: bfloat16 [64, 2, 256, 2048], P('ctx', None, None, 'tp'), may hold values from -6 to 6
- keys: bfloat16 [64, 2, 256, 512], P('ctx', None, None, 'tp'), may hold values from -6 to 6
- values: bfloat16 [64, 2, 256, 512], P('ctx', None, None, 'tp'), may hold values from -24 to 24
- column_block_table: int32 [4, 64], P('tp'), may hold values from 0 to 255, as said below
- slash_offsets: int32 [16, 64], P('tp'), may hold values from 1 to 256, as said below
- out_weight: bfloat16 [2048, 4096], P('tp'), may hold values from -0.125 to 0.125
Outputs:
- mixed: bfloat16 [64, 2, 256, 4096], P('ctx', None, None, 'tp')
Inputs may be any that keep to these rules, and one draw needn't show every extreme that they name: `column_block_table`: each row holds 64 distinct block numbers below 256, block b holding positions b * 128 to b * 128 + 127 and lying on the ctx device that holds its stretch. For each row, a quarter of the ctx devices hold exactly 2 of its blocks, half hold exactly one, the rest none. `slash_offsets`: each row holds 64 distinct offsets, and 1 and 256 are in every row.
All inputs are finite; a program needn't handle non-finite values.
Results may differ from a plain program's by a relative error of at most 0.00185.
The roundings to bfloat16 on the way count: a program that leaves them out, or rounds other values in their place, can miss the bound.
Values may be sent and summed in bfloat16 or wider, within the bound.
No kernel may reach another device: no remote copies, remote signals or barrier semaphores. Data moves between devices by JAX's collectives and lax.ppermute only.
A program may use at most 128 MiB of HBM per device.

v0:
```python
import jax
import jax.numpy as jnp
from jax import lax
from jax.sharding import PartitionSpec as P

HEAD_SIZE = 128
KEY_BLOCK_TOKENS = 128
CAP = 2


def passed_along(block, axis, distance):
    devices = range(lax.axis_size(axis))
    route = [(i - distance, i) for i in devices if i - distance in devices]
    return lax.ppermute(block, axis, route)


def owner_place(blocks, stretch_blocks, ctx_count):
    stretch_index = blocks // stretch_blocks
    first_half = stretch_index < ctx_count
    owner_device = jnp.where(first_half, stretch_index, 2 * ctx_count - 1 - stretch_index)
    local_index = jnp.where(first_half, 0, stretch_blocks) + blocks % stretch_blocks
    return (owner_device, local_index)


def slash_masks(offsets, stretch_len):
    span = 3 * stretch_len - 1
    relative = 2 * stretch_len - 1 - jnp.arange(span, dtype=jnp.int32)
    table = (
        jnp.any(relative[None, None, :] == offsets[:, :, None], axis=1) | (relative == 0)[None, :]
    )
    padded = jnp.concatenate([table, jnp.zeros((offsets.shape[0], 1), jnp.bool_)], axis=1)
    tiled = jnp.tile(padded, (1, stretch_len))[:, : stretch_len * span]
    rolled = tiled.reshape(offsets.shape[0], stretch_len, span)
    return rolled[:, :, stretch_len - 1 : 3 * stretch_len - 1]


def per_device(queries, keys, values, column_block_table, slash_offsets, out_weight):
    ctx_count = lax.axis_size("ctx")
    ctx_index = lax.axis_index("ctx")
    stretch_len = keys.shape[2]
    groups = keys.shape[3] // HEAD_SIZE
    heads = queries.shape[3] // HEAD_SIZE
    heads_per_group = heads // groups
    stretch_blocks = stretch_len // KEY_BLOCK_TOKENS
    listed = column_block_table.shape[1]
    scale = HEAD_SIZE ** (-0.5)
    kv_halves = jnp.stack([keys[0], values[0]], axis=1)
    local_blocks = kv_halves.reshape(2, 2, stretch_blocks, KEY_BLOCK_TOKENS, groups, HEAD_SIZE)
    local_blocks = local_blocks.transpose(4, 1, 0, 2, 3, 5).reshape(
        groups, 2, 2 * stretch_blocks, KEY_BLOCK_TOKENS, HEAD_SIZE
    )
    owner_device, local_index = owner_place(column_block_table, stretch_blocks, ctx_count)
    owned_here = owner_device == ctx_index
    same_owner = owner_device[:, :, None] == owner_device[:, None, :]
    position = jnp.arange(listed, dtype=jnp.int32)
    earlier = position[None, :] < position[:, None]
    owner_rank = jnp.sum(same_owner & earlier[None], axis=2)
    chosen_local = []
    chosen_valid = []
    for slot_rank in range(CAP):
        slot_hit = owned_here & (owner_rank == slot_rank)
        chosen_local.append(jnp.sum(jnp.where(slot_hit, local_index, 0), axis=1))
        chosen_valid.append(jnp.any(slot_hit, axis=1))
    chosen_local = jnp.stack(chosen_local, axis=1)
    chosen_valid = jnp.stack(chosen_valid, axis=1)
    outgoing = jnp.take_along_axis(local_blocks, chosen_local[:, None, :, None, None], axis=2)
    outgoing = jnp.where(
        chosen_valid[:, None, :, None, None], outgoing, jnp.zeros((), local_blocks.dtype)
    )
    arrived = lax.all_gather(outgoing, "ctx", axis=2, tiled=True)
    slot_index = owner_device * CAP + owner_rank
    column_kv = jnp.take_along_axis(arrived, slot_index[:, None, :, None, None], axis=2)
    before = passed_along(kv_halves[0], "ctx", 1)
    after = passed_along(kv_halves[1], "ctx", -1)
    after = jnp.where(ctx_index == ctx_count - 1, kv_halves[0], after)
    band_kv = jnp.concatenate([jnp.stack([before, after]), kv_halves], axis=2)
    stretch_ids = jnp.stack([ctx_index, 2 * ctx_count - 1 - ctx_index])
    query_pos = (
        stretch_ids[:, None] * stretch_len + jnp.arange(stretch_len, dtype=jnp.int32)[None, :]
    )
    flat_pos = query_pos.reshape(2 * stretch_len)
    band_pos = (stretch_ids[:, None] - 1) * stretch_len + jnp.arange(
        2 * stretch_len, dtype=jnp.int32
    )[None, :]
    band_listed = jnp.any(
        (band_pos // KEY_BLOCK_TOKENS)[None, :, :, None] == column_block_table[:, None, None, :],
        axis=3,
    )
    band_open = (band_pos >= 0)[None] & jnp.logical_not(band_listed)
    column_position = (
        column_block_table[:, :, None] * KEY_BLOCK_TOKENS
        + jnp.arange(KEY_BLOCK_TOKENS, dtype=jnp.int32)[None, None, :]
    ).reshape(groups, listed * KEY_BLOCK_TOKENS)
    slash_ok = slash_masks(slash_offsets, stretch_len)
    head_query = queries[0].reshape(2, stretch_len, heads, HEAD_SIZE).transpose(2, 0, 1, 3)
    column_keys = column_kv[:, 0].reshape(groups, listed * KEY_BLOCK_TOKENS, HEAD_SIZE)
    column_vals = column_kv[:, 1].reshape(groups, listed * KEY_BLOCK_TOKENS, HEAD_SIZE)
    band_keys = band_kv[:, 0].reshape(2, 2 * stretch_len, groups, HEAD_SIZE)
    band_vals = band_kv[:, 1].reshape(2, 2 * stretch_len, groups, HEAD_SIZE)

    def attend_head(inputs):
        one_query, one_slash, head_number = inputs
        group_number = head_number // heads_per_group
        keys_col = lax.dynamic_index_in_dim(column_keys, group_number, 0, keepdims=False)
        vals_col = lax.dynamic_index_in_dim(column_vals, group_number, 0, keepdims=False)
        keys_band = lax.dynamic_index_in_dim(band_keys, group_number, 2, keepdims=False)
        vals_band = lax.dynamic_index_in_dim(band_vals, group_number, 2, keepdims=False)
        open_band = lax.dynamic_index_in_dim(band_open, group_number, 0, keepdims=False)
        pos_col = lax.dynamic_index_in_dim(column_position, group_number, 0, keepdims=False)
        flat_query = one_query.reshape(2 * stretch_len, HEAD_SIZE)
        col_scores = (
            jnp.einsum("id,jd->ij", flat_query, keys_col, preferred_element_type=jnp.float32)
            * scale
        )
        col_mask = pos_col[None, :] <= flat_pos[:, None]
        band_scores = (
            jnp.einsum("hid,hjd->hij", one_query, keys_band, preferred_element_type=jnp.float32)
            * scale
        )
        band_mask = one_slash[None] & open_band[:, None, :]
        col_max = jnp.max(jnp.where(col_mask, col_scores, -jnp.inf), axis=1).reshape(2, stretch_len)
        band_max = jnp.max(jnp.where(band_mask, band_scores, -jnp.inf), axis=2)
        row_max = jnp.maximum(col_max, band_max)
        col_exp = jnp.where(
            col_mask, jnp.exp(col_scores - row_max.reshape(2 * stretch_len)[:, None]), 0.0
        )
        band_exp = jnp.where(band_mask, jnp.exp(band_scores - row_max[:, :, None]), 0.0)
        row_total = jnp.sum(col_exp, axis=1).reshape(2, stretch_len) + jnp.sum(band_exp, axis=2)
        weighted = jnp.dot(
            col_exp.astype(jnp.bfloat16), vals_col, preferred_element_type=jnp.float32
        ).reshape(2, stretch_len, HEAD_SIZE)
        weighted = weighted + jnp.einsum(
            "hij,hjd->hid",
            band_exp.astype(jnp.bfloat16),
            vals_band,
            preferred_element_type=jnp.float32,
        )
        return (weighted / row_total[:, :, None]).astype(jnp.bfloat16)

    head_out = lax.map(attend_head, (head_query, slash_ok, jnp.arange(heads, dtype=jnp.int32)))
    attended = head_out.transpose(1, 2, 0, 3).reshape(2, stretch_len, heads * HEAD_SIZE)
    partial_out = jnp.einsum(
        "hic,cd->hid", attended, out_weight, preferred_element_type=jnp.float32
    )
    mixed = lax.psum_scatter(partial_out, "tp", scatter_dimension=2, tiled=True).astype(
        jnp.bfloat16
    )
    return mixed[None]


def solution(mesh):
    in_specs = (
        P("ctx", None, None, "tp"),
        P("ctx", None, None, "tp"),
        P("ctx", None, None, "tp"),
        P("tp", None),
        P("tp", None),
        P("tp", None),
    )
    out_specs = P("ctx", None, None, "tp")
    return jax.shard_map(
        per_device, mesh=mesh, in_specs=in_specs, out_specs=out_specs, check_vma=False
    )
```

profile of v0, /device:TPU:1, one launch (start us, length us, event | category | flops | bytes accessed | tf_op | source)
XLA Modules:
  0.0 334.6 jit_solution(4886587028446778955)
XLA Ops:
  8.8 1.3 fusion.35
  10.1 1.3 compare_and_fusion
  11.4 1.0 pad_maximum_fusion
  13.0 1.4 add_bitcast_fusion.1
  16.1 5.1 %collective-permute-start.1 = (bf16[2,256,128]{2,1,0:T(8,128)(2,1)S(1)}, bf16[2,256,128]{2,1,0:T(8,128)(2,1)S(1)}, u32[]{:S(2)}, u32[]{:S(2)}) collective-permute-start(bf16[2,256,128]{2,1,0:T(8,128)(2,1)S(1)} %fusion.30), channel_id=1, source_target_pairs={{4,0},{8,4},{12,8},{16,12},{20,16},{24,20},{28,24},{32,28},{36,32}... | collective-permute-start | bytes 393224 | tf_op jit(solution)/shard_map/ppermute | solution.py:14
  24.5 0.9 select_bitcast_fusion
  25.4 1.9 collective-permute-start
  28.0 1.0 copy.51
  30.5 3.7 %reshape.503 = pred[4,256,767]{2,1,0:T(8,128)(4,1)S(1)} reshape(pred[785408]{0:T(1024)(128)(4,1)S(1)} %reshape.531) | data formatting | bytes 1570816 | tf_op jit(solution)/shard_map/reshape | solution.py:33
  34.9 1.2 copy.34
  36.8 0.9 maximum_maximum_fusion
  37.8 64.7 %all-gather.2.cloned.1.call-done = bf16[1,2,128,128,128]{4,3,1,0,2:T(8,128)(2,1)} async-done(((bf16[1,2,2,128,128]{4,3,1,0,2:T(8,128)(2,1)}), bf16[1,2,128,128,128]{4,3,1,0,2:T(8,128)(2,1)}) %all-gather.2.cloned.1.call-update) | async-done | bytes 8388624 | tf_op jit(solution)/shard_map/all_gather | solution.py:70
  102.5 10.3 %copy.55 = bf16[1,2,128,128,128]{4,3,2,1,0:T(8,128)(2,1)} copy(bf16[1,2,128,128,128]{4,3,1,0,2:T(8,128)(2,1)} %all-gather.2.cloned.1.call-done) | data formatting | bytes 16777216 | tf_op jit(solution)/shard_map/all_gather | solution.py:70
  112.9 6.4 %gather_fusion.1 = bf16[64,2,128,128]{3,2,1,0:T(8,128)(2,1)} fusion(bf16[2,128,128,128]{3,2,1,0:T(8,128)(2,1)} %bitcast.175, s32[1024]{0:T(1024)S(1)} %pad_clamp_fusion), kind=kCustom, calls=%fused_computation.1 | custom fusion | bytes 8388864 | tf_op jit(solution)/shard_map/jit(take_along_axis)/gather | solution.py:72
  119.3 2.6 bitcast_select_fusion
  121.9 2.5 fusion.41
  124.4 112.7 %while.12 = (s32[]{:T(128)}, bf16[4,2,256,128]{2,3,0,1:T(8,128)(2,1)S(1)}, bf16[4,2,256,128]{2,3,0,1:T(8,128)(2,1)S(1)}, bf16[1,8192,128]{2,1,0:T(8,128)(2,1)}, ...) while((s32[]{:T(128)}, ...), condition=%wide.region_12.13_spmd.clone, body=%wide.region_7.12_spmd.clone.sunk | while | flops 2326994944 | bytes 61042056 | solution.py:140
  125.3 8.7 %fusion.62 = (f32[512]{0:T(512)S(1)}, f32[512,8192]{1,0:T(8,128)}) fusion(s32[8192]{0:T(1024)S(1)} %bitcast.176, s32[512]{0:T(512)S(1)} %bitcast.194, bf16[512,128]{1,0:T(8,128)(2,1)S(1)} %bitcast.178, bf16[1,8192,128]{2,1,0:T(8,128)(2,1)} %get-tuple-element.312), kind=kOutput, calls=%fused_computation.6.clone.1 | convolution fusion | flops 1090518528 | bytes 19042304 | tf_op jit(solution)/shard_map/while/body/eval_jaxpr/id,jd->ij/dot_general | solution.py:112
  134.4 11.2 %fusion.64 = (f32[512]{0:T(512)S(1)}, bf16[512,8192]{1,0:T(8,128)(2,1)}) fusion(f32[512,8192]{1,0:T(8,128)} %get-tuple-element.279, f32[512]{0:T(512)S(1)} %max.19, s32[8192]{0:T(1024)S(1)} %bitcast.177, s32[512]{0:T(512)S(1)} %bitcast.195), kind=kLoop, calls=%fused_computation.7.clone.1 | loop fusion | flops 25165312 | bytes 25204736 | tf_op jit(solution)/shard_map/while/body/eval_jaxpr/reduce_sum | solution.py:128
  145.6 6.3 %fusion.65 = f32[2,256,128]{2,1,0:T(8,128)S(1)} fusion(bf16[2,256,8192]{2,1,0:T(8,128)(2,1)} %bitcast.174, bf16[1,8192,128]{2,1,0:T(8,128)(2,1)} %get-tuple-element.316), kind=kOutput, calls=%fused_computation.9.clone.1 | convolution fusion | flops 1073741824 | bytes 10747904 | tf_op jit(solution)/shard_map/while/body/eval_jaxpr/dot_general | solution.py:129
  153.4 8.7 %fusion.62 = (f32[512]{0:T(512)S(1)}, f32[512,8192]{1,0:T(8,128)}) fusion(s32[8192]{0:T(1024)S(1)} %bitcast.176, s32[512]{0:T(512)S(1)} %bitcast.194, bf16[512,128]{1,0:T(8,128)(2,1)S(1)} %bitcast.178, bf16[1,8192,128]{2,1,0:T(8,128)(2,1)} %get-tuple-element.312), kind=kOutput, calls=%fused_computation.6.clone.1 | convolution fusion | flops 1090518528 | bytes 19042304 | tf_op jit(solution)/shard_map/while/body/eval_jaxpr/id,jd->ij/dot_general | solution.py:112
  162.5 11.2 %fusion.64 = (f32[512]{0:T(512)S(1)}, bf16[512,8192]{1,0:T(8,128)(2,1)}) fusion(f32[512,8192]{1,0:T(8,128)} %get-tuple-element.279, f32[512]{0:T(512)S(1)} %max.19, s32[8192]{0:T(1024)S(1)} %bitcast.177, s32[512]{0:T(512)S(1)} %bitcast.195), kind=kLoop, calls=%fused_computation.7.clone.1 | loop fusion | flops 25165312 | bytes 25204736 | tf_op jit(solution)/shard_map/while/body/eval_jaxpr/reduce_sum | solution.py:128
  173.8 6.3 %fusion.65 = f32[2,256,128]{2,1,0:T(8,128)S(1)} fusion(bf16[2,256,8192]{2,1,0:T(8,128)(2,1)} %bitcast.174, bf16[1,8192,128]{2,1,0:T(8,128)(2,1)} %get-tuple-element.316), kind=kOutput, calls=%fused_computation.9.clone.1 | convolution fusion | flops 1073741824 | bytes 10747904 | tf_op jit(solution)/shard_map/while/body/eval_jaxpr/dot_general | solution.py:129
  181.6 8.7 %fusion.62 = (f32[512]{0:T(512)S(1)}, f32[512,8192]{1,0:T(8,128)}) fusion(s32[8192]{0:T(1024)S(1)} %bitcast.176, s32[512]{0:T(512)S(1)} %bitcast.194, bf16[512,128]{1,0:T(8,128)(2,1)S(1)} %bitcast.178, bf16[1,8192,128]{2,1,0:T(8,128)(2,1)} %get-tuple-element.312), kind=kOutput, calls=%fused_computation.6.clone.1 | convolution fusion | flops 1090518528 | bytes 19042304 | tf_op jit(solution)/shard_map/while/body/eval_jaxpr/id,jd->ij/dot_general | solution.py:112
  190.7 11.2 %fusion.64 = (f32[512]{0:T(512)S(1)}, bf16[512,8192]{1,0:T(8,128)(2,1)}) fusion(f32[512,8192]{1,0:T(8,128)} %get-tuple-element.279, f32[512]{0:T(512)S(1)} %max.19, s32[8192]{0:T(1024)S(1)} %bitcast.177, s32[512]{0:T(512)S(1)} %bitcast.195), kind=kLoop, calls=%fused_computation.7.clone.1 | loop fusion | flops 25165312 | bytes 25204736 | tf_op jit(solution)/shard_map/while/body/eval_jaxpr/reduce_sum | solution.py:128
  202.0 6.3 %fusion.65 = f32[2,256,128]{2,1,0:T(8,128)S(1)} fusion(bf16[2,256,8192]{2,1,0:T(8,128)(2,1)} %bitcast.174, bf16[1,8192,128]{2,1,0:T(8,128)(2,1)} %get-tuple-element.316), kind=kOutput, calls=%fused_computation.9.clone.1 | convolution fusion | flops 1073741824 | bytes 10747904 | tf_op jit(solution)/shard_map/while/body/eval_jaxpr/dot_general | solution.py:129
  209.8 8.7 %fusion.62 = (f32[512]{0:T(512)S(1)}, f32[512,8192]{1,0:T(8,128)}) fusion(s32[8192]{0:T(1024)S(1)} %bitcast.176, s32[512]{0:T(512)S(1)} %bitcast.194, bf16[512,128]{1,0:T(8,128)(2,1)S(1)} %bitcast.178, bf16[1,8192,128]{2,1,0:T(8,128)(2,1)} %get-tuple-element.312), kind=kOutput, calls=%fused_computation.6.clone.1 | convolution fusion | flops 1090518528 | bytes 19042304 | tf_op jit(solution)/shard_map/while/body/eval_jaxpr/id,jd->ij/dot_general | solution.py:112
  218.9 11.2 %fusion.64 = (f32[512]{0:T(512)S(1)}, bf16[512,8192]{1,0:T(8,128)(2,1)}) fusion(f32[512,8192]{1,0:T(8,128)} %get-tuple-element.279, f32[512]{0:T(512)S(1)} %max.19, s32[8192]{0:T(1024)S(1)} %bitcast.177, s32[512]{0:T(512)S(1)} %bitcast.195), kind=kLoop, calls=%fused_computation.7.clone.1 | loop fusion | flops 25165312 | bytes 25204736 | tf_op jit(solution)/shard_map/while/body/eval_jaxpr/reduce_sum | solution.py:128
  230.2 6.3 %fusion.65 = f32[2,256,128]{2,1,0:T(8,128)S(1)} fusion(bf16[2,256,8192]{2,1,0:T(8,128)(2,1)} %bitcast.174, bf16[1,8192,128]{2,1,0:T(8,128)(2,1)} %get-tuple-element.316), kind=kOutput, calls=%fused_computation.9.clone.1 | convolution fusion | flops 1073741824 | bytes 10747904 | tf_op jit(solution)/shard_map/while/body/eval_jaxpr/dot_general | solution.py:129
  237.1 7.8 %fusion.26 = f32[2,256,4096]{2,1,0:T(8,128)} fusion(bf16[2,256,512]{1,2,0:T(8,128)(2,1)S(1)} %bitcast.193, bf16[512,4096]{1,0:T(8,128)(2,1)} %param.13), kind=kOutput, calls=%fused_computation.38 | convolution fusion | flops 2147483648 | bytes 13107200 | tf_op jit(solution)/shard_map/hic,cd->hid/dot_general | solution.py:142
  244.9 80.2 %reduce-scatter.2.cloned.1.call-done = f32[2,256,1024]{2,1,0:T(8,128)} async-done(((f32[2,256,4096]{2,1,0:T(8,128)}), f32[2,256,1024]{2,1,0:T(8,128)}) %reduce-scatter.2.cloned.1.call-update) | async-done | bytes 2097168 | tf_op jit(solution)/shard_map/reduce_scatter | solution.py:145
  325.0 2.7 convert_bitcast_fusion
  (112 shorter events, 18.8 us)
Async XLA Ops:
  6.5 30.3 %copy-start.1 = (bf16[1,2,256,128]{3,2,1,0:T(8,128)(2,1)S(1)}, bf16[1,2,256,128]{3,2,1,0:T(8,128)(2,1)}, u32[]{:S(2)}) copy-start(bf16[1,2,256,128]{3,2,1,0:T(8,128)(2,1)} %param.9) | copy-start | bytes 393220
  6.5 30.3 %copy-start = (bf16[1,2,256,128]{3,2,1,0:T(8,128)(2,1)S(1)}, bf16[1,2,256,128]{3,2,1,0:T(8,128)(2,1)}, u32[]{:S(2)}) copy-start(bf16[1,2,256,128]{3,2,1,0:T(8,128)(2,1)} %param.10) | copy-start | bytes 393220
  6.5 96.0 %all-gather.2.cloned.1.call-start = ((), (), s32[]{:S(2)}) async-start(), calls=%async_computation.1 | async-start | bytes 8519680 | tf_op jit(solution)/shard_map/all_gather | solution.py:70
  15.1 309.9 %reduce-scatter.2.cloned.1.call-start = ((), (), s32[]{:S(2)}) async-start(), calls=%async_computation.2 | async-start | bytes 10485760 | tf_op jit(solution)/shard_map/reduce_scatter | solution.py:145
  16.1 8.4 %collective-permute-start.1 = (bf16[2,256,128]{2,1,0:T(8,128)(2,1)S(1)}, bf16[2,256,128]{2,1,0:T(8,128)(2,1)S(1)}, u32[]{:S(2)}, u32[]{:S(2)}) collective-permute-start(bf16[2,256,128]{2,1,0:T(8,128)(2,1)S(1)} %fusion.30), channel_id=1, source_target_pairs={{4,0},{8,4},{12,8},{16,12},{20,16},{24,20},{28,24},{32,28},{36,32}... | collective-permute-start | bytes 393224 | tf_op jit(solution)/shard_map/ppermute | solution.py:14
  25.4 11.4 %collective-permute-start = (bf16[2,256,128]{2,1,0:T(8,128)(2,1)S(1)}, bf16[2,256,128]{2,1,0:T(8,128)(2,1)}, u32[]{:S(2)}, u32[]{:S(2)}) collective-permute-start(bf16[2,256,128]{2,1,0:T(8,128)(2,1)S(1)} %get-tuple-element.185), channel_id=1, source_target_pairs={{0,4},{4,8},{8,12},{12,16},{16,20},{20,24},{24,28},{28,32},{32,36}... | collective-permute-start | bytes 393224 | tf_op jit(solution)/shard_map/ppermute | solution.py:14
  112.9 6.4 %copy-start.2 = (pred[64]{0:T(512)(128)(4,1)S(1)}, pred[64]{0:T(512)(128)(4,1)}, u32[]{:S(2)}) copy-start(pred[64]{0:T(512)(128)(4,1)} %compare_and_fusion.3) | copy-start | bytes 196
Sparse Core Ops, SparseCore 0:
  15.3 87.2 all-gather.1
  245.0 80.0 reduce-scatter.1
where the time goes:
time: 335 us
  waiting for transfers between devices  145 us (43%)
  matrix products  71.3 us (21%)
  other arithmetic  67.9 us (20%)
  local copies, waits for them, and re-layouts  29.5 us (9%)
  between operations  13.6 us (4%)
  starting transfers between devices  7.11 us (2%)
    reduce_scatter x1, waiting for transfers between devices, per_device(): lax.psum_scatter(partial_out, 'tp', scatter_dimension=2, tiled=True)  80.2 us
    all_gather x1, waiting for transfers between devices, per_device(): arrived = lax.all_gather(outgoing, 'ctx', axis=2, tiled=True)  64.7 us
    reduce_sum x4, other arithmetic, attend_head(): jnp.sum(col_exp, axis=1).reshape(2, stretch_len) + jnp.sum(band_exp, axis=2)  45 us
    dot_general x4, matrix products, attend_head(): jnp.einsum('id,jd->ij', flat_query, keys_col, preferred_element_type=jnp....  34.7 us
    dot_general x4, matrix products, attend_head(): jnp.dot(col_exp.astype(jnp.bfloat16), vals_col, preferred_element_type=jn...  25.2 us
    all_gather x1, local copies, waits for them, and re-layouts, per_device(): arrived = lax.all_gather(outgoing, 'ctx', axis=2, tiled=True)  10.3 us
    dot_general x1, matrix products, per_device(): jnp.einsum('hic,cd->hid', attended, out_weight, preferred_element_type=jn...  7.79 us
    ppermute x2, starting transfers between devices, passed_along(): return lax.ppermute(block, axis, route)  7.07 us
  transfers between devices with their start and end apart: 4, of which 2 were waited for; matrix products, arithmetic and copies ran while one was open for 5% of the time, Pallas kernels for 0%

commit v1 on v0

--- a/solution.py
+++ b/solution.py
@@ -6,6 +6,11 @@
 HEAD_SIZE = 128
 KEY_BLOCK_TOKENS = 128
 CAP = 2
+
+
+def gather_over(array, axis, dim):
+    outgoing = jnp.stack([array] * lax.axis_size(axis))
+    return jnp.concatenate(lax.all_to_all(outgoing, axis, 0, 0), axis=dim)
 
 
 def passed_along(block, axis, distance):
@@ -67,7 +72,7 @@
     outgoing = jnp.where(
         chosen_valid[:, None, :, None, None], outgoing, jnp.zeros((), local_blocks.dtype)
     )
-    arrived = lax.all_gather(outgoing, "ctx", axis=2, tiled=True)
+    arrived = gather_over(outgoing, "ctx", 2)
     slot_index = owner_device * CAP + owner_rank
     column_kv = jnp.take_along_axis(arrived, slot_index[:, None, :, None, None], axis=2)
     before = passed_along(kv_halves[0], "ctx", 1)

time: 335 us -> 464 us (1.39)
  waiting for transfers between devices: 145 us -> 262 us
  starting transfers between devices: 7.11 us -> 17.9 us
  local copies, waits for them, and re-layouts: 29.5 us -> 34.8 us
    ppermute x2, waiting for transfers between devices: 0.01 us -> 179 us  [passed_along(): return lax.ppermute(block, axis, route)]
    all_gather x1 -> x0, waiting for transfers between devices: 64.7 us -> none  [per_device(): arrived = lax.all_gather(outgoing, 'ctx', axis=2, tiled=True)]
    all_to_all x0 -> x1, starting transfers between devices: none -> 13.3 us  [gather_over(): return jnp.concatenate(lax.all_to_all(outgoing, axis, 0, 0), axis=dim)]
    all_to_all x0 -> x1, local copies, waits for them, and re-layouts: none -> 10.3 us  [gather_over(): return jnp.concatenate(lax.all_to_all(outgoing, axis, 0, 0), axis=dim)]
    all_gather x1 -> x0, local copies, waits for them, and re-layouts: 10.3 us -> none  [per_device(): arrived = lax.all_gather(outgoing, 'ctx', axis=2, tiled=True)]
    another operation x0 -> x1, local copies, waits for them, and re-layouts: none -> 5.34 us  [gather_over(): outgoing = jnp.stack([array] * lax.axis_size(axis))]
  transfers between devices with their start and end apart: 4 -> 4, of which waited for: 2 -> 2; matrix products, arithmetic and copies ran while one was open for 5% -> 3% of each run, Pallas kernels for 0% -> 0%
where the time goes in v1:
time: 464 us
  waiting for transfers between devices  262 us (56%)
  matrix products  71.3 us (15%)
  other arithmetic  63.4 us (14%)
  local copies, waits for them, and re-layouts  34.8 us (7%)
  starting transfers between devices  17.9 us (4%)
  between operations  13.7 us (3%)
    ppermute x2, waiting for transfers between devices, passed_along(): return lax.ppermute(block, axis, route)  179 us
    reduce_scatter x1, waiting for transfers between devices, per_device(): lax.psum_scatter(partial_out, 'tp', scatter_dimension=2, tiled=True)  82.8 us
    reduce_sum x4, other arithmetic, attend_head(): jnp.sum(col_exp, axis=1).reshape(2, stretch_len) + jnp.sum(band_exp, axis=2)  45 us
    dot_general x4, matrix products, attend_head(): jnp.einsum('id,jd->ij', flat_query, keys_col, preferred_element_type=jnp....  34.7 us
    dot_general x4, matrix products, attend_head(): jnp.dot(col_exp.astype(jnp.bfloat16), vals_col, preferred_element_type=jn...  25.2 us
    all_to_all x1, starting transfers between devices, gather_over(): return jnp.concatenate(lax.all_to_all(outgoing, axis, 0, 0), axis=dim)  13.3 us
    all_to_all x1, local copies, waits for them, and re-layouts, gather_over(): return jnp.concatenate(lax.all_to_all(outgoing, axis, 0, 0), axis=dim)  10.3 us
  transfers between devices with their start and end apart: 4, of which 2 were waited for; matrix products, arithmetic and copies ran while one was open for 3% of the time, Pallas kernels for 0%

profile of v1, /device:TPU:1, one launch (start us, length us, event | category | flops | bytes accessed | tf_op | source)
XLA Modules:
  0.0 463.7 jit_solution(7233577716543360393)
XLA Ops:
  8.8 1.3 fusion.33
  10.2 1.3 compare_and_fusion
  11.5 1.0 pad_maximum_fusion
  13.1 1.3 add_bitcast_fusion.1
  14.5 5.3 %stack.46 = bf16[64,1,2,2,128,128]{5,4,3,2,1,0:T(8,128)(2,1)} broadcast(bf16[2,2,128,128]{3,2,1,0:T(8,128)(2,1)S(1)} %copy.38), dimensions={2,3,4,5} | broadcast | bytes 8519680 | tf_op jit(solution)/shard_map/stack | solution.py:12
  19.9 13.3 %all-to-all-start = ((bf16[64,1,2,2,128,128]{5,4,3,2,1,0:T(8,128)(2,1)}), bf16[64,1,2,2,128,128]{5,4,3,2,1,0:T(8,128)(2,1)}, u32[]{:S(2)}, u32[]{:S(2)}) async-start(bf16[64,1,2,2,128,128]{5,4,3,2,1,0:T(8,128)(2,1)} %stack.46), calls=%async_computation | async-start | bytes 16777216 | tf_op jit(solution)/shard_map/all_to_all | solution.py:13
  33.3 2.4 collective-permute-start.1
  37.7 179.4 %collective-permute-done.1 = bf16[2,256,128]{2,1,0:T(8,128)(2,1)S(1)} collective-permute-done((bf16[2,256,128]{2,1,0:T(8,128)(2,1)S(1)}, bf16[2,256,128]{2,1,0:T(8,128)(2,1)S(1)}, u32[]{:S(2)}, u32[]{:S(2)}) %collective-permute-start.1) | collective-permute-done | bytes 131104 | tf_op jit(solution)/shard_map/ppermute | solution.py:19
  217.1 2.1 collective-permute-start
  219.2 1.0 copy.52
  221.7 3.7 reshape.509
  226.1 1.2 copy.35
  229.0 10.3 %copy.39 = bf16[64,1,2,2,128,128]{5,4,3,0,2,1:T(8,128)(2,1)} copy(bf16[64,1,2,2,128,128]{5,4,3,2,1,0:T(8,128)(2,1)} %all-to-all-done) | data formatting | bytes 16777216 | tf_op jit(solution)/shard_map/all_to_all | solution.py:13
  239.3 6.4 %gather_fusion.1 = bf16[64,2,128,128]{3,2,1,0:T(8,128)(2,1)} fusion(bf16[2,128,128,128]{3,2,1,0:T(8,128)(2,1)} %bitcast.167, s32[1024]{0:T(1024)S(1)} %pad_clamp_fusion), kind=kCustom, calls=%fused_computation.1 | custom fusion | bytes 8388864 | tf_op jit(solution)/shard_map/jit(take_along_axis)/gather | solution.py:77
  245.7 2.6 bitcast_select_fusion
  248.3 2.5 fusion.39
  250.8 112.7 %while.12 = (s32[]{:T(128)}, bf16[4,2,256,128]{2,3,0,1:T(8,128)(2,1)S(1)}, bf16[4,2,256,128]{2,3,0,1:T(8,128)(2,1)S(1)}, bf16[1,8192,128]{2,1,0:T(8,128)(2,1)}, ...) while((s32[]{:T(128)}, ...), condition=%wide.region_12.13_spmd.clone, body=%wide.region_7.12_spmd.clone.sunk | while | flops 2326994944 | bytes 61042056 | solution.py:145
  251.7 8.7 %fusion.60 = (f32[512]{0:T(512)S(1)}, f32[512,8192]{1,0:T(8,128)}) fusion(s32[8192]{0:T(1024)S(1)} %bitcast.168, s32[512]{0:T(512)S(1)} %bitcast.186, bf16[512,128]{1,0:T(8,128)(2,1)S(1)} %bitcast.170, bf16[1,8192,128]{2,1,0:T(8,128)(2,1)} %get-tuple-element.312), kind=kOutput, calls=%fused_computation.6.clone.1 | convolution fusion | flops 1090518528 | bytes 19042304 | tf_op jit(solution)/shard_map/while/body/eval_jaxpr/id,jd->ij/dot_general | solution.py:117
  260.8 11.2 %fusion.62 = (f32[512]{0:T(512)S(1)}, bf16[512,8192]{1,0:T(8,128)(2,1)}) fusion(f32[512,8192]{1,0:T(8,128)} %get-tuple-element.279, f32[512]{0:T(512)S(1)} %max.19, s32[8192]{0:T(1024)S(1)} %bitcast.169, s32[512]{0:T(512)S(1)} %bitcast.187), kind=kLoop, calls=%fused_computation.7.clone.1 | loop fusion | flops 25165312 | bytes 25204736 | tf_op jit(solution)/shard_map/while/body/eval_jaxpr/reduce_sum | solution.py:133
  272.1 6.3 %fusion.63 = f32[2,256,128]{2,1,0:T(8,128)S(1)} fusion(bf16[2,256,8192]{2,1,0:T(8,128)(2,1)} %bitcast.166, bf16[1,8192,128]{2,1,0:T(8,128)(2,1)} %get-tuple-element.316), kind=kOutput, calls=%fused_computation.9.clone.1 | convolution fusion | flops 1073741824 | bytes 10747904 | tf_op jit(solution)/shard_map/while/body/eval_jaxpr/dot_general | solution.py:134
  279.9 8.7 %fusion.60 = (f32[512]{0:T(512)S(1)}, f32[512,8192]{1,0:T(8,128)}) fusion(s32[8192]{0:T(1024)S(1)} %bitcast.168, s32[512]{0:T(512)S(1)} %bitcast.186, bf16[512,128]{1,0:T(8,128)(2,1)S(1)} %bitcast.170, bf16[1,8192,128]{2,1,0:T(8,128)(2,1)} %get-tuple-element.312), kind=kOutput, calls=%fused_computation.6.clone.1 | convolution fusion | flops 1090518528 | bytes 19042304 | tf_op jit(solution)/shard_map/while/body/eval_jaxpr/id,jd->ij/dot_general | solution.py:117
  289.0 11.2 %fusion.62 = (f32[512]{0:T(512)S(1)}, bf16[512,8192]{1,0:T(8,128)(2,1)}) fusion(f32[512,8192]{1,0:T(8,128)} %get-tuple-element.279, f32[512]{0:T(512)S(1)} %max.19, s32[8192]{0:T(1024)S(1)} %bitcast.169, s32[512]{0:T(512)S(1)} %bitcast.187), kind=kLoop, calls=%fused_computation.7.clone.1 | loop fusion | flops 25165312 | bytes 25204736 | tf_op jit(solution)/shard_map/while/body/eval_jaxpr/reduce_sum | solution.py:133
  300.3 6.3 %fusion.63 = f32[2,256,128]{2,1,0:T(8,128)S(1)} fusion(bf16[2,256,8192]{2,1,0:T(8,128)(2,1)} %bitcast.166, bf16[1,8192,128]{2,1,0:T(8,128)(2,1)} %get-tuple-element.316), kind=kOutput, calls=%fused_computation.9.clone.1 | convolution fusion | flops 1073741824 | bytes 10747904 | tf_op jit(solution)/shard_map/while/body/eval_jaxpr/dot_general | solution.py:134
  308.0 8.7 %fusion.60 = (f32[512]{0:T(512)S(1)}, f32[512,8192]{1,0:T(8,128)}) fusion(s32[8192]{0:T(1024)S(1)} %bitcast.168, s32[512]{0:T(512)S(1)} %bitcast.186, bf16[512,128]{1,0:T(8,128)(2,1)S(1)} %bitcast.170, bf16[1,8192,128]{2,1,0:T(8,128)(2,1)} %get-tuple-element.312), kind=kOutput, calls=%fused_computation.6.clone.1 | convolution fusion | flops 1090518528 | bytes 19042304 | tf_op jit(solution)/shard_map/while/body/eval_jaxpr/id,jd->ij/dot_general | solution.py:117
  317.2 11.2 %fusion.62 = (f32[512]{0:T(512)S(1)}, bf16[512,8192]{1,0:T(8,128)(2,1)}) fusion(f32[512,8192]{1,0:T(8,128)} %get-tuple-element.279, f32[512]{0:T(512)S(1)} %max.19, s32[8192]{0:T(1024)S(1)} %bitcast.169, s32[512]{0:T(512)S(1)} %bitcast.187), kind=kLoop, calls=%fused_computation.7.clone.1 | loop fusion | flops 25165312 | bytes 25204736 | tf_op jit(solution)/shard_map/while/body/eval_jaxpr/reduce_sum | solution.py:133
  328.4 6.3 %fusion.63 = f32[2,256,128]{2,1,0:T(8,128)S(1)} fusion(bf16[2,256,8192]{2,1,0:T(8,128)(2,1)} %bitcast.166, bf16[1,8192,128]{2,1,0:T(8,128)(2,1)} %get-tuple-element.316), kind=kOutput, calls=%fused_computation.9.clone.1 | convolution fusion | flops 1073741824 | bytes 10747904 | tf_op jit(solution)/shard_map/while/body/eval_jaxpr/dot_general | solution.py:134
  336.2 8.7 %fusion.60 = (f32[512]{0:T(512)S(1)}, f32[512,8192]{1,0:T(8,128)}) fusion(s32[8192]{0:T(1024)S(1)} %bitcast.168, s32[512]{0:T(512)S(1)} %bitcast.186, bf16[512,128]{1,0:T(8,128)(2,1)S(1)} %bitcast.170, bf16[1,8192,128]{2,1,0:T(8,128)(2,1)} %get-tuple-element.312), kind=kOutput, calls=%fused_computation.6.clone.1 | convolution fusion | flops 1090518528 | bytes 19042304 | tf_op jit(solution)/shard_map/while/body/eval_jaxpr/id,jd->ij/dot_general | solution.py:117
  345.3 11.2 %fusion.62 = (f32[512]{0:T(512)S(1)}, bf16[512,8192]{1,0:T(8,128)(2,1)}) fusion(f32[512,8192]{1,0:T(8,128)} %get-tuple-element.279, f32[512]{0:T(512)S(1)} %max.19, s32[8192]{0:T(1024)S(1)} %bitcast.169, s32[512]{0:T(512)S(1)} %bitcast.187), kind=kLoop, calls=%fused_computation.7.clone.1 | loop fusion | flops 25165312 | bytes 25204736 | tf_op jit(solution)/shard_map/while/body/eval_jaxpr/reduce_sum | solution.py:133
  356.6 6.3 %fusion.63 = f32[2,256,128]{2,1,0:T(8,128)S(1)} fusion(bf16[2,256,8192]{2,1,0:T(8,128)(2,1)} %bitcast.166, bf16[1,8192,128]{2,1,0:T(8,128)(2,1)} %get-tuple-element.316), kind=kOutput, calls=%fused_computation.9.clone.1 | convolution fusion | flops 1073741824 | bytes 10747904 | tf_op jit(solution)/shard_map/while/body/eval_jaxpr/dot_general | solution.py:134
  363.5 7.8 %fusion.26 = f32[2,256,4096]{2,1,0:T(8,128)} fusion(bf16[2,256,512]{1,2,0:T(8,128)(2,1)S(1)} %bitcast.185, bf16[512,4096]{1,0:T(8,128)(2,1)} %param.13), kind=kOutput, calls=%fused_computation.37 | convolution fusion | flops 2147483648 | bytes 13107200 | tf_op jit(solution)/shard_map/hic,cd->hid/dot_general | solution.py:147
  371.3 82.8 %reduce-scatter.2.cloned.1.call-done = f32[2,256,1024]{2,1,0:T(8,128)} async-done(((f32[2,256,4096]{2,1,0:T(8,128)}), f32[2,256,1024]{2,1,0:T(8,128)}) %reduce-scatter.2.cloned.1.call-update) | async-done | bytes 2097168 | tf_op jit(solution)/shard_map/reduce_scatter | solution.py:150
  454.1 2.7 convert_bitcast_fusion
  (117 shorter events, 16.2 us)
Async XLA Ops:
  19.9 13.4 %copy-start = (bf16[1,2,256,128]{3,2,1,0:T(8,128)(2,1)S(1)}, bf16[1,2,256,128]{3,2,1,0:T(8,128)(2,1)}, u32[]{:S(2)}) copy-start(bf16[1,2,256,128]{3,2,1,0:T(8,128)(2,1)} %param.10) | copy-start | bytes 393220
  19.9 13.4 %copy-start.1 = (bf16[1,2,256,128]{3,2,1,0:T(8,128)(2,1)S(1)}, bf16[1,2,256,128]{3,2,1,0:T(8,128)(2,1)}, u32[]{:S(2)}) copy-start(bf16[1,2,256,128]{3,2,1,0:T(8,128)(2,1)} %param.9) | copy-start | bytes 393220
  19.9 15.9 %copy-start.2 = (s32[4,64]{1,0:T(4,128)S(1)}, s32[4,64]{1,0:T(4,128)}, u32[]{:S(2)}) copy-start(s32[4,64]{1,0:T(4,128)} %param.12) | copy-start | bytes 3076
  19.9 16.3 %copy-start.4 = (s32[1,64]{1,0:T(1,128)S(1)}, s32[1,64]{1,0:T(1,128)}, u32[]{:S(2)}) copy-start(s32[1,64]{1,0:T(1,128)} %param.11) | copy-start | bytes 772
  19.9 209.1 %all-to-all-start = ((bf16[64,1,2,2,128,128]{5,4,3,2,1,0:T(8,128)(2,1)}), bf16[64,1,2,2,128,128]{5,4,3,2,1,0:T(8,128)(2,1)}, u32[]{:S(2)}, u32[]{:S(2)}) async-start(bf16[64,1,2,2,128,128]{5,4,3,2,1,0:T(8,128)(2,1)} %stack.46), calls=%async_computation | async-start | bytes 16777216 | tf_op jit(solution)/shard_map/all_to_all | solution.py:13
  33.2 420.9 %reduce-scatter.2.cloned.1.call-start = ((), (), s32[]{:S(2)}) async-start(), calls=%async_computation.2 | async-start | bytes 10485760 | tf_op jit(solution)/shard_map/reduce_scatter | solution.py:150
  33.3 183.8 %collective-permute-start.1 = (bf16[2,256,128]{2,1,0:T(8,128)(2,1)S(1)}, bf16[2,256,128]{2,1,0:T(8,128)(2,1)S(1)}, u32[]{:S(2)}, u32[]{:S(2)}) collective-permute-start(bf16[2,256,128]{2,1,0:T(8,128)(2,1)S(1)} %fusion.30), channel_id=1, source_target_pairs={{4,0},{8,4},{12,8},{16,12},{20,16},{24,20},{28,24},{32,28},{36,32}... | collective-permute-start | bytes 393224 | tf_op jit(solution)/shard_map/ppermute | solution.py:19
  217.1 10.9 %collective-permute-start = (bf16[2,256,128]{2,1,0:T(8,128)(2,1)S(1)}, bf16[2,256,128]{2,1,0:T(8,128)(2,1)}, u32[]{:S(2)}, u32[]{:S(2)}) collective-permute-start(bf16[2,256,128]{2,1,0:T(8,128)(2,1)S(1)} %get-tuple-element.185), channel_id=1, source_target_pairs={{0,4},{4,8},{8,12},{12,16},{16,20},{20,24},{24,28},{28,32},{32,36}... | collective-permute-start | bytes 393224 | tf_op jit(solution)/shard_map/ppermute | solution.py:19
  239.3 6.4 %copy-start.3 = (pred[64]{0:T(512)(128)(4,1)S(1)}, pred[64]{0:T(512)(128)(4,1)}, u32[]{:S(2)}) copy-start(pred[64]{0:T(512)(128)(4,1)} %compare_and_fusion.3) | copy-start | bytes 196
Sparse Core Ops, SparseCore 0:
  371.4 82.6 reduce-scatter.1
